TPU v7x, 32 devices: a whole 2x2x4 slice. The times are simulated.
32 devices in a mesh: batch: 4 (over y, x), ctx: 8 (over z, core).
Axes of the slice: x: 2, y: 2, z: 4, core: 2. Of those that a mesh axis runs over, the one named last changes fastest.
Arguments:
- inner_x: bfloat16 [4, 512, 8192], P('batch', 'ctx'), may hold values from -6 to 6
- inner_bc: bfloat16 [4, 512, 1024], P('batch', 'ctx'), may hold values from -6 to 6
- step_size: float32 [4, 512, 64], P('batch', 'ctx'), may hold values from 0.1 to 1400, as said below
- decay_base: float32 [64], replicated, may hold values from 0.9995 to 0.9998
- conv_inner: float32 [4, 8192], replicated, may hold values from -3 to 3
- conv_groups: float32 [4, 1024], replicated, may hold values from -3 to 3
- norm_gain: float32 [8192], replicated, may hold values from 0.5 to 1.5
- cache_pool: bfloat16 [16, 64, 128, 128], P('batch', 'ctx'), may hold values from -0.59765625 to 0.59765625
- reuse_owner: int32 [4], replicated, may hold values from 0 to 3
- reuse_level: int32 [4], replicated, may hold values from 0 to 4, as said below
- prompt_blocks: int32 [4], replicated, may hold values from 1 to 2
Outputs:
- mixer_out: bfloat16 [4, 512, 8192], P('batch', 'ctx')
Inputs may be any that keep to these rules, and one draw needn't show every extreme that they name: `step_size`: positive step sizes. `reuse_level`: 0 means nothing is cached; level l names the owner's l-th cached state.
All inputs are finite; a program needn't handle non-finite values.
Results may differ from a plain program's by a relative error of at most 0.009.
Values may be sent and summed in bfloat16 or wider, within the bound.
A program may use at most 64 MiB of HBM per device.

v0:
```python
import jax
import jax.numpy as jnp
from jax import lax
from jax.sharding import PartitionSpec as P

LOCAL_HEADS = 64
P_SIZE = 128
N = 128
GROUPS = 4
KCONV = 4
LEN_BLOCK = 256


def shifted(value, axis, steps):
    count = lax.axis_size(axis)
    first, last = (max(0, -steps), min(count, count - steps))
    return lax.ppermute(value, axis, [(source, source + steps) for source in range(first, last)])


def convolve(extended, weight, length):
    summed = jnp.zeros((length, extended.shape[1]), jnp.float32)
    for offset in range(weight.shape[0]):
        summed = summed + weight[offset] * extended[offset : offset + length].astype(jnp.float32)
    return jax.nn.silu(summed).astype(jnp.bfloat16)


def block_local(conv_x, write_proj, read_proj, log_step):
    length = log_step.shape[0]
    per_group = LOCAL_HEADS // GROUPS
    cumul = jnp.cumsum(log_step, axis=0)
    inject = -jnp.expm1(log_step)
    inner_heads = conv_x.reshape(length, GROUPS, per_group, P_SIZE)
    write_groups = write_proj.reshape(length, GROUPS, N)
    read_groups = read_proj.reshape(length, GROUPS, N)
    scores = jnp.einsum(
        "tgn,sgn->gts", read_groups, write_groups, preferred_element_type=jnp.float32
    )
    row_index = jnp.arange(length)[:, None]
    col_index = jnp.arange(length)[None, :]
    cumul_heads = cumul.T.reshape(GROUPS, per_group, length)
    inject_heads = inject.T.reshape(GROUPS, per_group, length)
    exponent_gap = cumul_heads[:, :, :, None] - cumul_heads[:, :, None, :]
    exponent_gap = jnp.where(row_index >= col_index, exponent_gap, -jnp.inf)
    mixing = (scores[:, None] * jnp.exp(exponent_gap) * inject_heads[:, :, None, :]).astype(
        jnp.bfloat16
    )
    intra_part = jnp.einsum(
        "gkts,sgkp->tgkp", mixing, inner_heads, preferred_element_type=jnp.float32
    )
    tail_weight = jnp.exp(cumul[-1][None, :] - cumul) * inject
    weighted = (inner_heads * tail_weight.reshape(length, GROUPS, per_group)[..., None]).astype(
        jnp.bfloat16
    )
    end_state = jnp.einsum(
        "sgkp,sgn->gkpn", weighted, write_groups, preferred_element_type=jnp.float32
    )
    end_state = end_state.reshape(LOCAL_HEADS, P_SIZE, N).astype(jnp.bfloat16)
    block_decay = jnp.exp(cumul[-1]).astype(jnp.bfloat16)
    return (intra_part.reshape(length, LOCAL_HEADS, P_SIZE), cumul, end_state, block_decay)


def block_output(intra_part, cumul, read_proj, incoming, norm_gain, live):
    length = cumul.shape[0]
    per_group = LOCAL_HEADS // GROUPS
    read_groups = read_proj.reshape(length, GROUPS, N)
    state_groups = incoming.reshape(GROUPS, per_group, P_SIZE, N)
    inter_part = jnp.einsum(
        "tgn,gkpn->tgkp", read_groups, state_groups, preferred_element_type=jnp.float32
    ).reshape(length, LOCAL_HEADS, P_SIZE)
    summed = intra_part + jnp.exp(cumul)[:, :, None] * inter_part
    inv_scale = lax.rsqrt(jnp.mean(summed * summed, axis=2, keepdims=True) + 1e-05)
    result = summed * inv_scale * norm_gain.reshape(LOCAL_HEADS, P_SIZE)
    result = jnp.where(live[:, None, None], result, 0.0)
    return result.reshape(length, LOCAL_HEADS * P_SIZE).astype(jnp.bfloat16)


def advance(running, pieces):
    decay_block, state_block = pieces
    next_state = decay_block.astype(jnp.float32)[:, None, None] * running + state_block.astype(
        jnp.float32
    )
    return (next_state, running)


def body(
    inner_x,
    inner_bc,
    step_size,
    decay_base,
    conv_inner,
    conv_groups,
    norm_gain,
    cache_pool,
    reuse_owner,
    reuse_level,
    prompt_blocks,
):
    length = inner_x.shape[1]
    width_x = inner_x.shape[2]
    request = lax.axis_index("batch")
    ctx_place = lax.axis_index("ctx")
    tail_rows = jnp.concatenate(
        [inner_x[0, length - KCONV + 1 :], inner_bc[0, length - KCONV + 1 :]], axis=1
    )
    tail_rows = shifted(tail_rows, "ctx", 1)
    conv_x = convolve(
        jnp.concatenate([tail_rows[:, :width_x], inner_x[0]], axis=0), conv_inner, length
    )
    conv_bc = convolve(
        jnp.concatenate([tail_rows[:, width_x:], inner_bc[0]], axis=0), conv_groups, length
    )
    positions = ctx_place * length + jnp.arange(length)
    live = positions < prompt_blocks[request] * LEN_BLOCK
    log_step = jnp.where(live[:, None], step_size[0], 0.0) * jnp.log(decay_base)[None, :]
    intra_part, cumul, end_state, block_decay = block_local(
        conv_x, conv_bc[:, : GROUPS * N], conv_bc[:, GROUPS * N :], log_step
    )
    cache_owner = reuse_owner[request]
    cached_level = reuse_level[request]
    slots = cache_pool.shape[0]
    pooled = lax.all_gather(cache_pool, "batch", axis=0, tiled=True)
    slot_index = cache_owner * slots + jnp.maximum(cached_level - 1, 0)
    start_state = lax.dynamic_index_in_dim(pooled, slot_index, 0, keepdims=False)
    start_state = jnp.where(cached_level > 0, start_state, jnp.zeros_like(start_state))
    ctx_count = lax.axis_size("ctx")
    head_share = LOCAL_HEADS // ctx_count
    decays_in, states_in = (
        lax.all_to_all(
            block_decay.reshape(ctx_count, head_share),
            "ctx",
            split_axis=0,
            concat_axis=0,
            tiled=True,
        ),
        lax.all_to_all(
            end_state.reshape(ctx_count, head_share, P_SIZE, N),
            "ctx",
            split_axis=0,
            concat_axis=0,
            tiled=True,
        ),
    )
    last_state, incoming_parts = lax.scan(
        advance, start_state.astype(jnp.float32), (decays_in, states_in)
    )
    returned = lax.all_to_all(
        incoming_parts.astype(jnp.bfloat16), "ctx", split_axis=0, concat_axis=0, tiled=True
    )
    incoming = returned.reshape(LOCAL_HEADS, P_SIZE, N)
    result = block_output(intra_part, cumul, conv_bc[:, GROUPS * N :], incoming, norm_gain, live)
    return result.reshape(1, length, LOCAL_HEADS * P_SIZE)


def solution(mesh):
    return jax.shard_map(
        body,
        mesh=mesh,
        in_specs=(
            P("batch", "ctx", None),
            P("batch", "ctx", None),
            P("batch", "ctx", None),
            P(),
            P(),
            P(),
            P(),
            P("batch", "ctx", None, None),
            P(),
            P(),
            P(),
        ),
        out_specs=P("batch", "ctx", None),
        check_vma=False,
    )
```

profile of v0, /device:TPU:0, one launch (start us, length us, event | category | flops | bytes accessed | tf_op | source)
XLA Modules:
  0.0 178.9 jit_solution(856277272822642632)
XLA Ops:
  6.5 0.7 all-gather.2.cloned.1.call-update
  7.3 0.9 slice_bitcast_fusion
  8.2 0.7 slice_bitcast_fusion.1
  9.0 2.4 %collective-permute-start = (bf16[3,9216]{1,0:T(4,128)(2,1)S(1)}, bf16[3,9216]{1,0:T(4,128)(2,1)S(1)}, u32[]{:S(2)}, u32[]{:S(2)}) collective-permute-start(bf16[3,9216]{1,0:T(4,128)(2,1)S(1)} %pad_maximum_fusion.2), channel_id=1, source_target_pairs={{0,1},{1,2},{2,3},{3,4},{4,5},{5,6},{6,7},{8,9},{9,10},{10,11},{11... | collective-permute-start | bytes 165896 | tf_op jit(solution)/shard_map/ppermute | solution.py:17
  11.3 0.8 copy.48
  12.2 0.7 log.3
  12.8 1.2 dynamic_slice.21
  14.8 0.1 exponential-minus-one_negate_fusion
  14.9 0.1 copy.49
  14.9 0.1 reduce_window_sum.13
  15.1 0.7 convert_element_type.119
  15.8 6.2 %all-to-all-start = ((bf16[8,1,8]{2,1,0:T(2,128)(2,1)}), bf16[8,1,8]{2,1,0:T(2,128)(2,1)S(1)}, u32[]{:S(2)}, u32[]{:S(2)}) async-start(bf16[8,1,8]{2,1,0:T(2,128)(2,1)} %convert_element_type.119), calls=%async_computation | async-start | bytes 8192 | tf_op jit(solution)/shard_map/all_to_all | solution.py:128
  21.9 0.1 copy.55
  22.0 0.1 mul.260
  22.1 0.1 sub.37
  22.2 0.1 fusion.33
  22.3 1.3 fusion.32
  23.6 0.0 collective-permute-done
  23.6 0.2 multiply_convert_fusion.5
  23.9 1.6 fusion.16
  25.5 0.3 copy.70
  25.8 0.0 copy-start
  25.8 1.0 copy-done
  26.8 3.4 %convolution_convert_fusion = bf16[4,16,128,128]{3,2,1,0:T(8,128)(2,1)} fusion(f32[64,4,16]{0,2,1:T(8,128)S(1)} %get-tuple-element.54, bf16[64,4,16,128]{3,2,1,0:T(8,128)(2,1)S(1)} %bitcast.84, bf16[64,4,128,1]{2,1,0,3:T(4,128)(2,1)S(1)} %bitcast.90), kind=kOutput, calls=%fused_computation.12 | convolution fusion | flops 136839168 | bytes 3227648 | tf_op jit(solution)/shard_map/sgkp,sgn->gkpn/dot_general | solution.py:54
  30.2 0.0 all-to-all-done
  30.2 5.2 %all-to-all-start.1 = ((bf16[8,8,128,128]{3,2,1,0:T(8,128)(2,1)}), bf16[8,8,128,128]{3,2,1,0:T(8,128)(2,1)S(1)}, u32[]{:S(2)}, u32[]{:S(2)}) async-start(bf16[8,8,128,128]{3,2,1,0:T(8,128)(2,1)} %bitcast.28), calls=%async_computation.1 | async-start | bytes 4194304 | tf_op jit(solution)/shard_map/all_to_all | solution.py:135
  35.4 0.6 dynamic_slice.22
  37.3 0.6 dynamic_slice.23
  38.6 26.1 %all-gather.2.cloned.1.call-done = bf16[16,8,128,128]{3,2,1,0:T(8,128)(2,1)} async-done(((bf16[4,8,128,128]{3,2,1,0:T(8,128)(2,1)}), bf16[16,8,128,128]{3,2,1,0:T(8,128)(2,1)}) %all-gather.2.cloned.1.call-update) | async-done | bytes 4194320 | tf_op jit(solution)/shard_map/all_gather | solution.py:121
  64.6 1.0 bitcast_convert_fusion
  65.6 18.9 %all-to-all-done.1 = bf16[8,8,128,128]{3,2,1,0:T(8,128)(2,1)S(1)} async-done(((bf16[8,8,128,128]{3,2,1,0:T(8,128)(2,1)}), bf16[8,8,128,128]{3,2,1,0:T(8,128)(2,1)S(1)}, u32[]{:S(2)}, u32[]{:S(2)}) %all-to-all-start.1) | async-done | bytes 2097184 | tf_op jit(solution)/shard_map/all_to_all | solution.py:135
  84.5 7.4 %while.12 = (s32[]{:T(128)}, f32[8,128,128]{2,1,0:T(8,128)S(1)}, bf16[8,8,128,128]{3,2,1,0:T(8,128)(2,1)}, bf16[8,8]{1,0:T(8,128)(2,1)S(1)}, bf16[8,8,128,128]{3,2,1,0:T(8,128)(2,1)S(1)}, /*index=5*/s32[]{:T(128)}) while((s32[]{:T(128)}, f32[8,128,128]{2,1,0:T(8,128)S(1)}, bf16[8,8,128,128]{3,2,1,0:T(8,128)(2,1)}, bf16[8,8]{1,0:T(8,128)(2,1)S(1)}, ...), condition=%wide.region_2.3_spmd, body=%wide.region_1.2_spmd.sunk | while | flops 393226 | bytes 2359965 | solution.py:143
  84.5 0.7 bitcast_dynamic-update-slice_fusion.2
  85.2 0.2 convert_add_fusion.2
  85.4 0.7 bitcast_dynamic-update-slice_fusion.2
  86.2 0.2 convert_add_fusion.2
  86.3 0.8 bitcast_dynamic-update-slice_fusion.2
  87.1 0.2 convert_add_fusion.2
  87.3 0.7 bitcast_dynamic-update-slice_fusion.2
  88.0 0.2 convert_add_fusion.2
  88.2 0.8 bitcast_dynamic-update-slice_fusion.2
  89.0 0.2 convert_add_fusion.2
  89.1 0.8 bitcast_dynamic-update-slice_fusion.2
  89.9 0.2 convert_add_fusion.2
  90.1 0.8 bitcast_dynamic-update-slice_fusion.2
  90.8 0.2 convert_add_fusion.2
  91.0 0.7 bitcast_dynamic-update-slice_fusion.2
  91.8 0.2 convert_add_fusion.2
  91.9 4.4 %all-to-all-start.2 = ((bf16[8,8,128,128]{3,2,1,0:T(8,128)(2,1)}), bf16[8,8,128,128]{3,2,1,0:T(8,128)(2,1)}, u32[]{:S(2)}, u32[]{:S(2)}) async-start(bf16[8,8,128,128]{3,2,1,0:T(8,128)(2,1)} %get-tuple-element.32), calls=%async_computation.2 | async-start | bytes 4194304 | tf_op jit(solution)/shard_map/all_to_all | solution.py:146
  96.3 0.1 copy.50
  96.4 1.9 %mul.257 = f32[64,64,128]{2,1,0:T(8,128)} broadcast(f32[64,64]{1,0:T(8,128)S(1)} %exp.43), dimensions={0,1} | broadcast | bytes 2113536 | tf_op jit(solution)/shard_map/mul | solution.py:70
  98.3 1.7 mul.258
  100.1 0.1 fusion.21
  100.2 45.1 %all-to-all-done.2 = bf16[8,8,128,128]{3,2,1,0:T(8,128)(2,1)} async-done(((bf16[8,8,128,128]{3,2,1,0:T(8,128)(2,1)}), bf16[8,8,128,128]{3,2,1,0:T(8,128)(2,1)}, u32[]{:S(2)}, u32[]{:S(2)}) %all-to-all-start.2) | async-done | bytes 2097184 | tf_op jit(solution)/shard_map/all_to_all | solution.py:146
  145.3 2.4 %fusion.4 = f32[64,4,16,128]{3,0,2,1:T(8,128)S(1)} fusion(bf16[64,4,128,1]{2,1,0,3:T(4,128)(2,1)S(1)} %bitcast.89, bf16[4,16,128,128]{3,2,1,0:T(8,128)(2,1)} %bitcast.77), kind=kOutput, calls=%fused_computation.13 | convolution fusion | flops 134217728 | bytes 4259840 | tf_op jit(solution)/shard_map/tgn,gkpn->tgkp/dot_general | solution.py:67
  147.8 2.5 %copy.59 = f32[64,4,16,128]{3,2,1,0:T(8,128)} copy(f32[64,4,16,128]{3,0,2,1:T(8,128)S(1)} %fusion.4) | data formatting | bytes 4194304 | tf_op jit(solution)/shard_map/tgn,gkpn->tgkp/transpose | solution.py:67
  150.3 3.0 %multiply_reduce_fusion = (f32[64,4,16]{0,2,1:T(8,128)S(1)}, f32[64,4,16,128]{3,0,2,1:T(8,128)}) fusion(f32[64,4,16,128]{3,0,2,1:T(8,128)S(1)} %fusion.4, f32[64,4,16]{0,2,1:T(8,128)S(1)} %get-tuple-element.53, bf16[64,4,16,128]{3,2,1,0:T(8,128)(2,1)S(1)} %bitcast.85, f32[4,16,64]{2,1,0:T(8,128)S(1)} %bitcast.98, f32[4,16,64]{2,1,0:T(8,128)S(1)} %bitcast.99, ...), kind=kOutput, calls=%fused_computation.8 | convolution fusion | flops 70512640 | bytes 5378048 | tf_op jit(solution)/shard_map/gkts,sgkp->tgkp/dot_general | solution.py:47
  153.3 0.1 copy.60
  153.4 2.0 %mul.270 = f32[64,64,128]{2,1,0:T(8,128)} broadcast(f32[64,64]{1,0:T(8,128)S(1)} %copy.60), dimensions={0,1} | broadcast | bytes 2113536 | tf_op jit(solution)/shard_map/mul | solution.py:72
  155.4 2.7 %mul.271 = f32[1,64,8192]{2,1,0:T(8,128)} reshape(f32[64,64,128]{2,1,0:T(8,128)} %mul.270) | data formatting | bytes 4194304 | tf_op jit(solution)/shard_map/mul | solution.py:72
  158.1 4.2 %copy.52 = f32[64,4,16,128]{3,2,1,0:T(8,128)} copy(f32[64,4,16,128]{3,0,2,1:T(8,128)} %get-tuple-element.60) | data formatting | bytes 4194304 | tf_op jit(solution)/shard_map/gkts,sgkp->tgkp/transpose | solution.py:47
  162.3 2.8 %reshape.233 = f32[1,64,8192]{2,1,0:T(8,128)} reshape(f32[64,4,16,128]{3,2,1,0:T(8,128)} %copy.52) | data formatting | bytes 4194304 | tf_op jit(solution)/shard_map/reshape | solution.py:59
  165.0 2.8 %reshape.234 = f32[1,64,8192]{2,1,0:T(8,128)} reshape(f32[64,4,16,128]{3,2,1,0:T(8,128)} %copy.59) | data formatting | bytes 4194304 | tf_op jit(solution)/shard_map/reshape | solution.py:69
  167.8 4.3 %select_convert_fusion = bf16[1,64,8192]{2,1,0:T(8,128)(2,1)} fusion(f32[1,64,8192]{2,1,0:T(8,128)} %mul.271, f32[1,64,8192]{2,1,0:T(8,128)} %reshape.233, f32[1,64,8192]{2,1,0:T(8,128)S(1)} %mul.258, f32[1,64,8192]{2,1,0:T(8,128)} %reshape.234, f32[8192]{0:T(1024)S(1)} %copy-done.4, pred[64]{0:T(512)(128)(4,1)S(1)} %add_compare_fusion), kind=kLoop, calls=%fused_computation.7 | loop fusion | flops 3145728 | bytes 9470016 | tf_op jit(solution)/shard_map/convert_element_type | solution.py:74
  (38 shorter events, 0.3 us)
Async XLA Ops:
  6.5 17.4 %copy-start.2 = (bf16[1,64,8192]{2,1,0:T(8,128)(2,1)S(1)}, bf16[1,64,8192]{2,1,0:T(8,128)(2,1)}, u32[]{:S(2)}) copy-start(bf16[1,64,8192]{2,1,0:T(8,128)(2,1)} %param.13) | copy-start | bytes 3145732
  6.5 17.1 %copy-start.3 = (bf16[1,64,1024]{2,1,0:T(8,128)(2,1)S(1)}, bf16[1,64,1024]{2,1,0:T(8,128)(2,1)}, u32[]{:S(2)}) copy-start(bf16[1,64,1024]{2,1,0:T(8,128)(2,1)} %param.14) | copy-start | bytes 393220
  6.5 17.0 %copy-start.5 = (f32[4,1024]{1,0:T(4,128)S(1)}, f32[4,1024]{1,0:T(4,128)}, u32[]{:S(2)}) copy-start(f32[4,1024]{1,0:T(4,128)} %param.18) | copy-start | bytes 49156
  6.5 58.1 %all-gather.2.cloned.1.call-start = ((), (), s32[]{:S(2)}) async-start(), calls=%async_computation.3 | async-start | bytes 5242880 | tf_op jit(solution)/shard_map/all_gather | solution.py:121
  9.0 14.6 %collective-permute-start = (bf16[3,9216]{1,0:T(4,128)(2,1)S(1)}, bf16[3,9216]{1,0:T(4,128)(2,1)S(1)}, u32[]{:S(2)}, u32[]{:S(2)}) collective-permute-start(bf16[3,9216]{1,0:T(4,128)(2,1)S(1)} %pad_maximum_fusion.2), channel_id=1, source_target_pairs={{0,1},{1,2},{2,3},{3,4},{4,5},{5,6},{6,7},{8,9},{9,10},{10,11},{11... | collective-permute-start | bytes 165896 | tf_op jit(solution)/shard_map/ppermute | solution.py:17
  15.8 14.4 %all-to-all-start = ((bf16[8,1,8]{2,1,0:T(2,128)(2,1)}), bf16[8,1,8]{2,1,0:T(2,128)(2,1)S(1)}, u32[]{:S(2)}, u32[]{:S(2)}) async-start(bf16[8,1,8]{2,1,0:T(2,128)(2,1)} %convert_element_type.119), calls=%async_computation | async-start | bytes 8192 | tf_op jit(solution)/shard_map/all_to_all | solution.py:128
  25.8 1.0 copy-start
  30.2 5.2 %copy-start.6 = (s32[4]{0:T(128)S(1)}, s32[4]{0:T(128)}, u32[]{:S(2)}) copy-start(s32[4]{0:T(128)} %param.22) | copy-start | bytes 52
  30.2 7.1 %copy-start.7 = (s32[4]{0:T(128)S(1)}, s32[4]{0:T(128)}, u32[]{:S(2)}) copy-start(s32[4]{0:T(128)} %param.21) | copy-start | bytes 52
  30.2 54.3 %all-to-all-start.1 = ((bf16[8,8,128,128]{3,2,1,0:T(8,128)(2,1)}), bf16[8,8,128,128]{3,2,1,0:T(8,128)(2,1)S(1)}, u32[]{:S(2)}, u32[]{:S(2)}) async-start(bf16[8,8,128,128]{3,2,1,0:T(8,128)(2,1)} %bitcast.28), calls=%async_computation.1 | async-start | bytes 4194304 | tf_op jit(solution)/shard_map/all_to_all | solution.py:135
  91.9 53.4 %all-to-all-start.2 = ((bf16[8,8,128,128]{3,2,1,0:T(8,128)(2,1)}), bf16[8,8,128,128]{3,2,1,0:T(8,128)(2,1)}, u32[]{:S(2)}, u32[]{:S(2)}) async-start(bf16[8,8,128,128]{3,2,1,0:T(8,128)(2,1)} %get-tuple-element.32), calls=%async_computation.2 | async-start | bytes 4194304 | tf_op jit(solution)/shard_map/all_to_all | solution.py:146
  147.8 2.6 %copy-start.1 = (bf16[8,8,64,128]{3,2,1,0:T(8,128)(2,1)S(1)}, bf16[8,8,64,128]{3,2,1,0:T(8,128)(2,1)}, u32[]{:S(2)}) copy-start(bf16[8,8,64,128]{3,2,1,0:T(8,128)(2,1)} %copy-done) | copy-start | bytes 3145732
  165.0 2.8 %copy-start.4 = (f32[8192]{0:T(1024)S(1)}, f32[8192]{0:T(1024)}, u32[]{:S(2)}) copy-start(f32[8192]{0:T(1024)} %param.19) | copy-start | bytes 98308
Sparse Core Ops, SparseCore 0:
  9.2 55.3 all-gather.1
where the time goes:
time: 180 us; the launch traced here: 179 us
  waiting for transfers between devices  90.8 us (50%)
  local copies, waits for them, and re-layouts  36 us (20%)
  starting transfers between devices  18.1 us (10%)
  between operations  16.2 us (9%)
  matrix products  9.01 us (5%)
  other arithmetic  8.74 us (5%)
    all_to_all x1, waiting for transfers between devices, body(): lax.all_to_all(incoming_parts.astype(jnp.bfloat16), 'ctx', split_axis=0,...  45.1 us
    all_gather x1, waiting for transfers between devices, body(): pooled = lax.all_gather(cache_pool, 'batch', axis=0, tiled=True)  26.1 us
    all_to_all x1, waiting for transfers between devices, body(): lax.all_to_all(end_state.reshape(ctx_count, head_share, P_SIZE, N), 'ctx'...  18.9 us
    all_to_all x1, starting transfers between devices, body(): lax.all_to_all(block_decay.reshape(ctx_count, head_share), 'ctx', split_a...  6.16 us
    dynamic_update_slice x8, local copies, waits for them, and re-layouts, body(): lax.scan(advance, start_state.astype(jnp.float32), (decays_in, states_in))  5.97 us
    all_to_all x1, starting transfers between devices, body(): lax.all_to_all(end_state.reshape(ctx_count, head_share, P_SIZE, N), 'ctx'...  5.24 us
    mul x2, local copies, waits for them, and re-layouts, block_output(): result = summed * inv_scale * norm_gain.reshape(LOCAL_HEADS, P_SIZE)  4.69 us
    all_to_all x1, starting transfers between devices, body(): lax.all_to_all(incoming_parts.astype(jnp.bfloat16), 'ctx', split_axis=0,...  4.35 us
  transfers between devices with their start and end apart: 5, of which 3 were waited for; matrix products, arithmetic and copies ran while one was open for 10% of the time, Pallas kernels for 0%

commit v1 on v0

v1 whole, which is shorter than its diff:
```python
import functools

import jax
import jax.numpy as jnp
from jax import lax
from jax.experimental import pallas as pl
from jax.experimental.pallas import tpu as pltpu
from jax.sharding import PartitionSpec as P

LOCAL_HEADS = 64
P_SIZE = 128
N = 128
GROUPS = 4
KCONV = 4
LEN_BLOCK = 256
HALO = 16
F32 = jnp.float32
BF16 = jnp.bfloat16
MESH = pl.DeviceIdType.MESH
NT = (((1,), (1,)), ((), ()))
TN = (((0,), (0,)), ((), ()))


def one_minus_exp(value):
    total = jnp.ones_like(value)
    for term in range(12, 1, -1):
        total = 1.0 + value * (1.0 / term) * total
    return -value * total


def convolved(ext_ref, weight, length, width):
    summed = jnp.zeros((length, width), F32)
    for offset in range(KCONV):
        start = 8 - (KCONV - 1) + offset
        summed = summed + weight[offset : offset + 1] * ext_ref[start : start + length, :width]
    return (summed * jax.nn.sigmoid(summed)).astype(BF16)


def kernel(
    nb, nc, length,
    owner_ref, level_ref, blocks_ref,
    x_ref, bc_ref, step_ref, stept_ref, base_ref, baset_ref, wx_ref, wbc_ref, gain_ref, pool_ref,
    out_ref,
    hx, hbc, ext, bcv, colc, coli, rowc, rowi, intra, ends, inc, nxt, sel_out, sel_in, start,
    halo_send, halo_recv, sel_send, sel_recv, st_send, inc_recv, nxt_send,
):
    hs = LOCAL_HEADS // nc
    width = hs * P_SIZE
    per_group = LOCAL_HEADS // GROUPS
    me_b = lax.axis_index("batch")
    me_c = lax.axis_index("ctx")
    live_count = blocks_ref[me_b] * LEN_BLOCK

    barrier = pltpu.get_barrier_semaphore()
    for step in range(1, nb):
        pl.semaphore_signal(barrier, inc=1, device_id=(lax.rem(me_b + step, nb), me_c), device_id_type=MESH)
    for step in range(1, nc):
        pl.semaphore_signal(barrier, inc=1, device_id=(me_b, lax.rem(me_c + step, nc)), device_id_type=MESH)

    def pick(request):
        return pool_ref[jnp.maximum(level_ref[request] - 1, 0)].reshape(width, N)

    for step in range(1, nb):
        sel_out[step - 1] = pick(lax.rem(me_b + step, nb))
    own = pick(me_b)
    pl.semaphore_wait(barrier, nb - 1 + nc - 1)

    def halo_copy(which):
        source, target = ((x_ref, hx), (bc_ref, hbc))[which]
        return pltpu.make_async_remote_copy(
            src_ref=source.at[pl.ds(length - HALO, HALO)], dst_ref=target,
            send_sem=halo_send.at[which], recv_sem=halo_recv.at[which],
            device_id=(me_b, lax.rem(me_c + 1, nc)), device_id_type=MESH,
        )

    def sel_copy(step):
        return pltpu.make_async_remote_copy(
            src_ref=sel_out.at[step - 1], dst_ref=sel_in.at[step - 1],
            send_sem=sel_send.at[step - 1], recv_sem=sel_recv.at[step - 1],
            device_id=(lax.rem(me_b + step, nb), me_c), device_id_type=MESH,
        )

    def start_copy():
        return pltpu.make_async_remote_copy(
            src_ref=start, dst_ref=inc.at[me_c],
            send_sem=st_send, recv_sem=inc_recv.at[me_c],
            device_id=(me_b, 0), device_id_type=MESH,
        )

    def next_copy(k):
        return pltpu.make_async_remote_copy(
            src_ref=nxt.at[k], dst_ref=inc.at[k],
            send_sem=nxt_send.at[k], recv_sem=inc_recv.at[k],
            device_id=(me_b, lax.rem(me_c + 1, nc)), device_id_type=MESH,
        )

    @pl.when(me_c < nc - 1)
    def _():
        halo_copy(1).start()
        halo_copy(0).start()

    for step in range(1, nb):
        sel_copy(step).start()

    first = me_c * length
    row_at = lax.broadcasted_iota(jnp.int32, (length, LOCAL_HEADS), 0)
    col_at = lax.broadcasted_iota(jnp.int32, (LOCAL_HEADS, length), 1)
    logs = jnp.where(first + row_at < live_count, step_ref[...], 0.0) * jnp.log(base_ref[...])
    logst = jnp.where(first + col_at < live_count, stept_ref[...], 0.0) * jnp.log(baset_ref[...])
    at_t = lax.broadcasted_iota(jnp.int32, (length, length), 0)
    at_s = lax.broadcasted_iota(jnp.int32, (length, length), 1)
    causal = at_t >= at_s
    lower = causal.astype(F32)
    upper = (at_t <= at_s).astype(F32)
    cum = jnp.dot(lower, logs, precision=lax.Precision.HIGHEST, preferred_element_type=F32)
    cumt = jnp.dot(logst, upper, precision=lax.Precision.HIGHEST, preferred_element_type=F32)
    tail = jnp.exp(cum[length - 1 : length] - cum) * one_minus_exp(logs)
    injt = one_minus_exp(logst)
    for k in range(nc):
        colc[k] = cum[:, k * hs : (k + 1) * hs]
        coli[k] = tail[:, k * hs : (k + 1) * hs]
        rowc[k] = cumt[k * hs : (k + 1) * hs]
        rowi[k] = injt[k * hs : (k + 1) * hs]

    @pl.when(me_c == 0)
    def _():
        hx[...] = jnp.zeros_like(hx)
        hbc[...] = jnp.zeros_like(hbc)

    @pl.when(me_c > 0)
    def _():
        halo_copy(1).wait_recv()
        halo_copy(0).wait_recv()

    half = GROUPS * N
    for part in range(2):
        cols = slice(part * half, (part + 1) * half)
        for piece in range(GROUPS):
            at = part * half + piece * N
            ext[0:8, :N] = hbc[:, at : at + N].astype(F32)[HALO - 8 :]
            ext[8 : 8 + length, :N] = bc_ref[:, at : at + N].astype(F32)
            bcv[part * GROUPS + piece] = convolved(ext, wbc_ref[:, at : at + N], length, N)

    def local_part(k, carry):
        group = k * hs // per_group
        cols = pl.ds(pl.multiple_of(k * width, 128), width)
        write = bcv[group]
        read = bcv[GROUPS + group]
        scores = lax.dot_general(read, write, NT, preferred_element_type=F32)
        col_c, col_i, row_c, row_i = colc[k], coli[k], rowc[k], rowi[k]
        ext[0:8, :width] = hx[:, cols].astype(F32)[HALO - 8 :]
        ext[8 : 8 + length, :width] = x_ref[:, cols].astype(F32)
        conv = convolved(ext, wx_ref[:, cols], length, width)
        outs, weighted = [], []
        for j in range(hs):
            head = conv[:, j * P_SIZE : (j + 1) * P_SIZE]
            gap = jnp.where(causal, col_c[:, j : j + 1] - row_c[j : j + 1], -jnp.inf)
            mixing = (scores * jnp.exp(gap) * row_i[j : j + 1]).astype(BF16)
            outs.append(jnp.dot(mixing, head, preferred_element_type=F32))
            weighted.append((head.astype(F32) * col_i[:, j : j + 1]).astype(BF16))
        intra[k] = jnp.concatenate(outs, axis=1)
        stacked = jnp.concatenate(weighted, axis=1)
        ends[k] = lax.dot_general(stacked, write, TN, preferred_element_type=F32).astype(BF16)
        return carry

    lax.fori_loop(0, nc, local_part, 0)

    owner = owner_ref[me_b]
    level = level_ref[me_b]
    state = jnp.where(owner == me_b, own, jnp.zeros_like(own))
    for step in range(1, nb):
        sel_copy(step).wait_recv()
        state = jnp.where(owner == lax.rem(me_b + nb - step, nb), sel_in[step - 1], state)
    state = jnp.where(level > 0, state, jnp.zeros_like(state))

    @pl.when(me_c == 0)
    def _():
        inc[0] = state

    @pl.when(me_c > 0)
    def _():
        start[...] = state
        start_copy().start()

    def chain_part(k, carry):
        @pl.when(me_c + k > 0)
        def _():
            next_copy(k).wait_recv()

        row_c = rowc[k]
        decay = jnp.exp(row_c[:, length - 1 : length]).astype(BF16).astype(F32)

        @pl.when(me_c < nc - 1)
        def _():
            for j in range(hs):
                rows = slice(j * P_SIZE, (j + 1) * P_SIZE)
                nxt[k, rows] = (
                    decay[j : j + 1] * inc[k, rows].astype(F32) + ends[k, rows].astype(F32)
                ).astype(BF16)
            next_copy(k).start()

        cols = pl.ds(pl.multiple_of(k * width, 128), width)
        read = bcv[GROUPS + k * hs // per_group]
        inter = lax.dot_general(read, inc[k], NT, preferred_element_type=F32)
        grown = jnp.exp(colc[k])
        gain = gain_ref[:, cols]
        alive = first + lax.broadcasted_iota(jnp.int32, (length, P_SIZE), 0) < live_count
        outs = []
        for j in range(hs):
            lanes = slice(j * P_SIZE, (j + 1) * P_SIZE)
            summed = intra[k, :, lanes] + grown[:, j : j + 1] * inter[:, lanes]
            scale = lax.rsqrt(jnp.mean(summed * summed, axis=1, keepdims=True) + 1e-05)
            outs.append(jnp.where(alive, summed * scale * gain[:, lanes], 0.0).astype(BF16))
        out_ref[:, cols] = jnp.concatenate(outs, axis=1)
        return carry

    lax.fori_loop(0, nc, chain_part, 0)

    for step in range(1, nb):
        sel_copy(step).wait_send()

    @pl.when(me_c > 0)
    def _():
        start_copy().wait_send()

    @pl.when(me_c < nc - 1)
    def _():
        halo_copy(1).wait_send()
        halo_copy(0).wait_send()

        def drain(k, carry):
            next_copy(k).wait_send()
            return carry

        lax.fori_loop(0, nc, drain, 0)


def body(
    nb, nc,
    inner_x, inner_bc, step_size, decay_base, conv_inner, conv_groups, norm_gain, cache_pool,
    reuse_owner, reuse_level, prompt_blocks,
):
    length, width_x = inner_x.shape[1:]
    width_bc = inner_bc.shape[2]
    hs = LOCAL_HEADS // nc
    width = hs * P_SIZE
    smem = pl.BlockSpec(memory_space=pltpu.SMEM)
    vmem = pl.BlockSpec(memory_space=pltpu.VMEM)
    dma = pltpu.SemaphoreType.DMA
    result = pl.pallas_call(
        functools.partial(kernel, nb, nc, length),
        out_shape=jax.ShapeDtypeStruct((length, width_x), BF16),
        in_specs=[smem] * 3 + [vmem] * 10,
        out_specs=vmem,
        scratch_shapes=[
            pltpu.VMEM((HALO, width_x), BF16),
            pltpu.VMEM((HALO, width_bc), BF16),
            pltpu.VMEM((8 + length, max(width, N)), F32),
            pltpu.VMEM((2 * GROUPS, length, N), BF16),
            pltpu.VMEM((nc, length, hs), F32),
            pltpu.VMEM((nc, length, hs), F32),
            pltpu.VMEM((nc, hs, length), F32),
            pltpu.VMEM((nc, hs, length), F32),
            pltpu.VMEM((nc, length, width), F32),
            pltpu.VMEM((nc, width, N), BF16),
            pltpu.VMEM((nc, width, N), BF16),
            pltpu.VMEM((nc, width, N), BF16),
            pltpu.VMEM((nb - 1, width, N), BF16),
            pltpu.VMEM((nb - 1, width, N), BF16),
            pltpu.VMEM((width, N), BF16),
            dma((2,)),
            dma((2,)),
            dma((nb - 1,)),
            dma((nb - 1,)),
            dma,
            dma((nc,)),
            dma((nc,)),
        ],
        compiler_params=pltpu.CompilerParams(
            collective_id=0, has_side_effects=True, vmem_limit_bytes=40 * 1024 * 1024
        ),
    )(
        reuse_owner, reuse_level, prompt_blocks,
        inner_x[0], inner_bc[0], step_size[0], step_size[0].T,
        decay_base[None, :], decay_base[:, None], conv_inner, conv_groups, norm_gain[None, :],
        cache_pool,
    )
    return result[None]


def solution(mesh):
    return jax.shard_map(
        functools.partial(body, mesh.shape["batch"], mesh.shape["ctx"]),
        mesh=mesh,
        in_specs=(
            P("batch", "ctx", None),
            P("batch", "ctx", None),
            P("batch", "ctx", None),
            P(),
            P(),
            P(),
            P(),
            P("batch", "ctx", None, None),
            P(),
            P(),
            P(),
        ),
        out_specs=P("batch", "ctx", None),
        check_vma=False,
    )
```

time: 180 us -> 78 us (0.43)
  the two profiles are of different devices: /device:TPU:0 before, /device:TPU:25 now
where the time goes in v1:
time: 78 us; the launch traced here: 77.6 us
  Pallas kernels  70.8 us (91%)
  local copies, waits for them, and re-layouts  6.76 us (9%)
    pallas_call x1, Pallas kernels, body(): pl.pallas_call(functools.partial(kernel, nb, nc, length), out_shape=jax.S...  70.8 us
    unnamed x24, local copies, waits for them, and re-layouts  6.01 us

profile of v1, /device:TPU:25, one launch (start us, length us, event | category | flops | bytes accessed | tf_op | source)
XLA Modules:
  0.0 77.6 jit_solution(177956243830735241)
XLA Ops:
  0.0 0.0 copy-start.2
  0.0 0.8 copy.14.baset_ref
  0.8 0.0 copy-done.2
  0.8 0.0 copy-start.5
  0.8 0.0 copy-start.6
  0.8 0.0 copy-start.10
  0.8 0.1 copy.12
  0.9 0.0 copy-start.7
  0.9 0.0 copy-start.8
  0.9 0.0 copy-start.9
  0.9 0.6 copy-done.5
  1.5 0.0 copy-done.6
  1.5 0.0 copy-done.10
  1.5 0.0 copy-done.7
  1.5 0.0 copy-done.8
  1.5 0.0 copy-done.9
  1.6 0.0 copy-start
  1.6 1.2 %copy-done = bf16[1,64,8192]{2,1,0:T(8,128)(2,1)S(1)} copy-done((bf16[1,64,8192]{2,1,0:T(8,128)(2,1)S(1)}, bf16[1,64,8192]{2,1,0:T(8,128)(2,1)}, u32[]{:S(2)}) %copy-start) | copy-done | bytes 1048600
  2.8 0.0 copy-start.1
  2.8 1.2 %copy-done.1 = bf16[4,8,128,128]{3,2,1,0:T(8,128)(2,1)S(1)} copy-done((bf16[4,8,128,128]{3,2,1,0:T(8,128)(2,1)S(1)}, bf16[4,8,128,128]{3,2,1,0:T(8,128)(2,1)}, u32[]{:S(2)}) %copy-start.1) | copy-done | bytes 1048600
  4.0 0.0 copy-start.3
  4.0 0.9 %copy-done.3 = bf16[1,64,1024]{2,1,0:T(8,128)(2,1)S(1)} copy-done((bf16[1,64,1024]{2,1,0:T(8,128)(2,1)S(1)}, bf16[1,64,1024]{2,1,0:T(8,128)(2,1)}, u32[]{:S(2)}) %copy-start.3) | copy-done | bytes 131096
  4.9 0.0 copy-start.4
  4.9 0.9 %copy-done.4 = f32[4,8192]{1,0:T(4,128)S(1)} copy-done((f32[4,8192]{1,0:T(4,128)S(1)}, f32[4,8192]{1,0:T(4,128)}, u32[]{:S(2)}) %copy-start.4) | copy-done | bytes 131096
  5.8 70.8 %shard_map.109 = bf16[64,8192]{1,0:T(8,128)(2,1)S(1)} custom-call(s32[4]{0:T(128)S(1)} %copy-done.8, s32[4]{0:T(128)S(1)} %copy-done.9, s32[4]{0:T(128)S(1)} %copy-done.10, bf16[64,8192]{1,0:T(8,128)(2,1)S(1)} %bitcast.11, bf16[64,1024]{1,0:T(8,128)(2,1)S(1)} %bitcast.14, f32[64,64]{1,0:T(8,128)S(1)} %bitcast.12, f32[64,64]{1,0:T(8,128)S(1)} %bitcast.13, ...), custom_call_target="tpu_custom_call" | custom-call | tf_op jit(solution)/shard_map/pallas_call | solution.py:250
  76.6 1.0 %copy.17 = bf16[1,64,8192]{2,1,0:T(8,128)(2,1)} copy(bf16[1,64,8192]{2,1,0:T(8,128)(2,1)S(1)} %bitcast.10) | data formatting | bytes 2097152
Async XLA Ops:
  0.0 0.8 copy-start.2
  0.8 0.8 copy-start.5
  0.8 0.8 copy-start.6
  0.8 0.8 copy-start.10
  0.9 0.7 copy-start.7
  0.9 0.7 copy-start.8
  0.9 0.7 copy-start.9
  1.6 1.2 %copy-start = (bf16[1,64,8192]{2,1,0:T(8,128)(2,1)S(1)}, bf16[1,64,8192]{2,1,0:T(8,128)(2,1)}, u32[]{:S(2)}) copy-start(bf16[1,64,8192]{2,1,0:T(8,128)(2,1)} %param.11) | copy-start | bytes 3145732
  2.8 1.2 %copy-start.1 = (bf16[4,8,128,128]{3,2,1,0:T(8,128)(2,1)S(1)}, bf16[4,8,128,128]{3,2,1,0:T(8,128)(2,1)}, u32[]{:S(2)}) copy-start(bf16[4,8,128,128]{3,2,1,0:T(8,128)(2,1)} %pool_ref.1) | copy-start | bytes 3145732
  4.0 0.9 %copy-start.3 = (bf16[1,64,1024]{2,1,0:T(8,128)(2,1)S(1)}, bf16[1,64,1024]{2,1,0:T(8,128)(2,1)}, u32[]{:S(2)}) copy-start(bf16[1,64,1024]{2,1,0:T(8,128)(2,1)} %param.12) | copy-start | bytes 393220
  4.9 0.9 %copy-start.4 = (f32[4,8192]{1,0:T(4,128)S(1)}, f32[4,8192]{1,0:T(4,128)}, u32[]{:S(2)}) copy-start(f32[4,8192]{1,0:T(4,128)} %wx_ref.1) | copy-start | bytes 393220

commit v2 on v1

v2 whole, which is shorter than its diff:
```python
import functools

import jax
import jax.numpy as jnp
from jax import lax
from jax.experimental import pallas as pl
from jax.experimental.pallas import tpu as pltpu
from jax.sharding import PartitionSpec as P

LOCAL_HEADS = 64
P_SIZE = 128
N = 128
GROUPS = 4
KCONV = 4
LEN_BLOCK = 256
HALO = 16
PARTS = 2
F32 = jnp.float32
BF16 = jnp.bfloat16
MESH = pl.DeviceIdType.MESH
NT = (((1,), (1,)), ((), ()))
TN = (((0,), (0,)), ((), ()))


def one_minus_exp(value):
    total = jnp.ones_like(value)
    for term in range(12, 1, -1):
        total = 1.0 + value * (1.0 / term) * total
    return -value * total


def convolved(ext_ref, weight, length, width):
    summed = jnp.zeros((length, width), F32)
    for offset in range(KCONV):
        start = 8 - (KCONV - 1) + offset
        summed = summed + weight[offset : offset + 1] * ext_ref[start : start + length, :width]
    return (summed * jax.nn.sigmoid(summed)).astype(BF16)


def kernel(
    nb, nc, length,
    owner_ref, level_ref, blocks_ref,
    x_hbm, bc_ref, step_ref, base_ref, wx_hbm, wbc_ref, gain_ref, pool_hbm,
    out_ref,
    x_ref, wx_ref, pool_ref, convs,
    hx, hbc, ext, bcv, colc, coli, rowc, rowi, intra, ends, inc, nxt, sel_out, sel_in, start,
    local_sem, halo_send, halo_recv, sel_send, sel_recv, st_send, inc_recv, nxt_send,
):
    hs = LOCAL_HEADS // nc
    width = hs * P_SIZE
    sub = width // PARTS
    per_group = LOCAL_HEADS // GROUPS
    me_b = lax.axis_index("batch")
    me_c = lax.axis_index("ctx")
    live_count = blocks_ref[me_b] * LEN_BLOCK

    loads = [
        pltpu.make_async_copy(source, target, local_sem.at[at])
        for at, (source, target) in enumerate(((pool_hbm, pool_ref), (x_hbm, x_ref), (wx_hbm, wx_ref)))
    ]
    for load in loads:
        load.start()
    barrier = pltpu.get_barrier_semaphore()
    for step in range(1, nb):
        pl.semaphore_signal(barrier, inc=1, device_id=(lax.rem(me_b + step, nb), me_c), device_id_type=MESH)
    for step in range(1, nc):
        pl.semaphore_signal(barrier, inc=1, device_id=(me_b, lax.rem(me_c + step, nc)), device_id_type=MESH)

    loads[0].wait()

    def pick(request):
        return pool_ref[jnp.maximum(level_ref[request] - 1, 0)].reshape(width, N)

    for step in range(1, nb):
        sel_out[step - 1] = pick(lax.rem(me_b + step, nb))
    start[...] = pick(me_b)
    loads[1].wait()
    pl.semaphore_wait(barrier, nb - 1 + nc - 1)

    def halo_copy(which):
        source, target = ((x_ref, hx), (bc_ref, hbc))[which]
        return pltpu.make_async_remote_copy(
            src_ref=source.at[pl.ds(length - HALO, HALO)], dst_ref=target,
            send_sem=halo_send.at[which], recv_sem=halo_recv.at[which],
            device_id=(me_b, lax.rem(me_c + 1, nc)), device_id_type=MESH,
        )

    def sel_copy(step):
        return pltpu.make_async_remote_copy(
            src_ref=sel_out.at[step - 1], dst_ref=sel_in.at[step - 1],
            send_sem=sel_send.at[step - 1], recv_sem=sel_recv.at[step - 1],
            device_id=(lax.rem(me_b + step, nb), me_c), device_id_type=MESH,
        )

    def start_copy(part):
        rows = pl.ds(part * sub, sub)
        return pltpu.make_async_remote_copy(
            src_ref=start.at[rows], dst_ref=inc.at[me_c, rows],
            send_sem=st_send.at[part], recv_sem=inc_recv.at[me_c, part],
            device_id=(me_b, 0), device_id_type=MESH,
        )

    def next_copy(k, part):
        rows = pl.ds(part * sub, sub)
        return pltpu.make_async_remote_copy(
            src_ref=nxt.at[k, rows], dst_ref=inc.at[k, rows],
            send_sem=nxt_send.at[k, part], recv_sem=inc_recv.at[k, part],
            device_id=(me_b, lax.rem(me_c + 1, nc)), device_id_type=MESH,
        )

    @pl.when(me_c < nc - 1)
    def _():
        halo_copy(1).start()
        halo_copy(0).start()

    for step in range(1, nb):
        sel_copy(step).start()

    first = me_c * length
    row_at = lax.broadcasted_iota(jnp.int32, (length, LOCAL_HEADS), 0)
    logs = jnp.where(first + row_at < live_count, step_ref[...], 0.0) * jnp.log(base_ref[...])
    at_t = lax.broadcasted_iota(jnp.int32, (length, length), 0)
    at_s = lax.broadcasted_iota(jnp.int32, (length, length), 1)
    causal = at_t >= at_s
    lower = causal.astype(F32)
    upper = (at_t <= at_s).astype(F32)
    cum = jnp.dot(lower, logs, precision=lax.Precision.HIGHEST, preferred_element_type=F32)
    cumt = lax.dot_general(logs, upper, TN, precision=lax.Precision.HIGHEST, preferred_element_type=F32)
    inject = one_minus_exp(logs)
    tail = jnp.exp(cum[length - 1 : length] - cum) * inject
    same = (at_t == at_s).astype(F32)
    injt = lax.dot_general(inject, same, TN, precision=lax.Precision.HIGHEST, preferred_element_type=F32)
    for k in range(nc):
        colc[k] = cum[:, k * hs : (k + 1) * hs]
        coli[k] = tail[:, k * hs : (k + 1) * hs]
        rowc[k] = cumt[k * hs : (k + 1) * hs]
        rowi[k] = injt[k * hs : (k + 1) * hs]

    @pl.when(me_c == 0)
    def _():
        hx[...] = jnp.zeros_like(hx)
        hbc[...] = jnp.zeros_like(hbc)

    @pl.when(me_c > 0)
    def _():
        halo_copy(1).wait_recv()
        halo_copy(0).wait_recv()

    half = GROUPS * N
    for part in range(2):
        cols = slice(part * half, (part + 1) * half)
        for piece in range(GROUPS):
            at = part * half + piece * N
            ext[0:8, :N] = hbc[:, at : at + N].astype(F32)[HALO - 8 :]
            ext[8 : 8 + length, :N] = bc_ref[:, at : at + N].astype(F32)
            bcv[part * GROUPS + piece] = convolved(ext, wbc_ref[:, at : at + N], length, N)

    loads[2].wait()

    def columns(k):
        return pl.ds(pl.multiple_of(k * width, 128), width)

    def end_part(k):
        col_i = coli[k]
        ext[0:8, :width] = hx[:, columns(k)].astype(F32)[HALO - 8 :]
        ext[8 : 8 + length, :width] = x_ref[:, columns(k)].astype(F32)
        conv = convolved(ext, wx_ref[:, columns(k)], length, width)
        convs[k] = conv
        weighted = [
            (conv[:, j * P_SIZE : (j + 1) * P_SIZE].astype(F32) * col_i[:, j : j + 1]).astype(BF16)
            for j in range(hs)
        ]
        stacked = jnp.concatenate(weighted, axis=1)
        write = bcv[k * hs // per_group]
        ends[k] = lax.dot_general(stacked, write, TN, preferred_element_type=F32).astype(BF16)

    def intra_part(k):
        group = k * hs // per_group
        scores = lax.dot_general(bcv[GROUPS + group], bcv[group], NT, preferred_element_type=F32)
        col_c, row_c, row_i = colc[k], rowc[k], rowi[k]
        for j in range(hs):
            lanes = slice(j * P_SIZE, (j + 1) * P_SIZE)
            gap = jnp.where(causal, col_c[:, j : j + 1] - row_c[j : j + 1], -jnp.inf)
            mixing = (scores * jnp.exp(gap) * row_i[j : j + 1]).astype(BF16)
            intra[k, :, lanes] = jnp.dot(mixing, convs[k, :, lanes], preferred_element_type=F32)

    def start_part():
        owner = owner_ref[me_b]
        level = level_ref[me_b]
        for step in range(1, nb):
            sel_copy(step).wait_recv()
        state = jnp.where(owner == me_b, start[...], jnp.zeros_like(start))
        for step in range(1, nb):
            state = jnp.where(owner == lax.rem(me_b + nb - step, nb), sel_in[step - 1], state)
        state = jnp.where(level > 0, state, jnp.zeros_like(state))

        @pl.when(me_c == 0)
        def _():
            inc[0] = state

        @pl.when(me_c > 0)
        def _():
            start[...] = state
            for part in range(PARTS):
                start_copy(part).start()

    def chain_part(k):
        decay = jnp.exp(rowc[k][:, length - 1 : length]).astype(BF16).astype(F32)
        for part in range(PARTS):
            @pl.when(me_c + k > 0)
            def _():
                next_copy(k, part).wait_recv()

            @pl.when(me_c < nc - 1)
            def _():
                for j in range(part * hs // PARTS, (part + 1) * hs // PARTS):
                    rows = slice(j * P_SIZE, (j + 1) * P_SIZE)
                    nxt[k, rows] = (
                        decay[j : j + 1] * inc[k, rows].astype(F32) + ends[k, rows].astype(F32)
                    ).astype(BF16)
                next_copy(k, part).start()

    def out_part(k):
        read = bcv[GROUPS + k * hs // per_group]
        inter = lax.dot_general(read, inc[k], NT, preferred_element_type=F32)
        grown = jnp.exp(colc[k])
        gain = gain_ref[:, columns(k)]
        alive = first + lax.broadcasted_iota(jnp.int32, (length, P_SIZE), 0) < live_count
        outs = []
        for j in range(hs):
            lanes = slice(j * P_SIZE, (j + 1) * P_SIZE)
            summed = intra[k, :, lanes] + grown[:, j : j + 1] * inter[:, lanes]
            scale = lax.rsqrt(jnp.mean(summed * summed, axis=1, keepdims=True) + 1e-05)
            outs.append(jnp.where(alive, summed * scale * gain[:, lanes], 0.0).astype(BF16))
        out_ref[:, columns(k)] = jnp.concatenate(outs, axis=1)

    start_at = jnp.where(me_c == 0, 0, nc // 2 - 1)

    def ends_step(k, carry):
        end_part(k)
        pl.when(k == start_at)(start_part)

        @pl.when(me_c == 0)
        def _():
            chain_part(k)

        return carry

    def intra_step(k, carry):
        intra_part(k)
        return carry

    def late_step(k, carry):
        @pl.when(me_c > 0)
        def _():
            chain_part(k)

        @pl.when(me_c < 2)
        def _():
            intra_part(k)

        out_part(k)
        return carry

    lax.fori_loop(0, nc, ends_step, 0)

    @pl.when(me_c >= 2)
    def _():
        lax.fori_loop(0, nc, intra_step, 0)

    lax.fori_loop(0, nc, late_step, 0)

    for step in range(1, nb):
        sel_copy(step).wait_send()

    @pl.when(me_c > 0)
    def _():
        for part in range(PARTS):
            start_copy(part).wait_send()

    @pl.when(me_c < nc - 1)
    def _():
        halo_copy(1).wait_send()
        halo_copy(0).wait_send()

        def drain(k, carry):
            for part in range(PARTS):
                next_copy(k, part).wait_send()
            return carry

        lax.fori_loop(0, nc, drain, 0)


def body(
    nb, nc,
    inner_x, inner_bc, step_size, decay_base, conv_inner, conv_groups, norm_gain, cache_pool,
    reuse_owner, reuse_level, prompt_blocks,
):
    length, width_x = inner_x.shape[1:]
    width_bc = inner_bc.shape[2]
    hs = LOCAL_HEADS // nc
    width = hs * P_SIZE
    smem = pl.BlockSpec(memory_space=pltpu.SMEM)
    vmem = pl.BlockSpec(memory_space=pltpu.VMEM)
    hbm = pl.BlockSpec(memory_space=pl.ANY)
    dma = pltpu.SemaphoreType.DMA
    result = pl.pallas_call(
        functools.partial(kernel, nb, nc, length),
        out_shape=jax.ShapeDtypeStruct((length, width_x), BF16),
        in_specs=[smem] * 3 + [hbm, vmem, vmem, vmem, hbm, vmem, vmem, hbm],
        out_specs=vmem,
        scratch_shapes=[
            pltpu.VMEM((length, width_x), BF16),
            pltpu.VMEM((KCONV, width_x), F32),
            pltpu.VMEM(cache_pool.shape, BF16),
            pltpu.VMEM((nc, length, width), BF16),
            pltpu.VMEM((HALO, width_x), BF16),
            pltpu.VMEM((HALO, width_bc), BF16),
            pltpu.VMEM((8 + length, max(width, N)), F32),
            pltpu.VMEM((2 * GROUPS, length, N), BF16),
            pltpu.VMEM((nc, length, hs), F32),
            pltpu.VMEM((nc, length, hs), F32),
            pltpu.VMEM((nc, hs, length), F32),
            pltpu.VMEM((nc, hs, length), F32),
            pltpu.VMEM((nc, length, width), F32),
            pltpu.VMEM((nc, width, N), BF16),
            pltpu.VMEM((nc, width, N), BF16),
            pltpu.VMEM((nc, width, N), BF16),
            pltpu.VMEM((nb - 1, width, N), BF16),
            pltpu.VMEM((nb - 1, width, N), BF16),
            pltpu.VMEM((width, N), BF16),
            dma((3,)),
            dma((2,)),
            dma((2,)),
            dma((nb - 1,)),
            dma((nb - 1,)),
            dma((PARTS,)),
            dma((nc, PARTS)),
            dma((nc, PARTS)),
        ],
        compiler_params=pltpu.CompilerParams(
            collective_id=0, has_side_effects=True, vmem_limit_bytes=56 * 1024 * 1024
        ),
    )(
        reuse_owner, reuse_level, prompt_blocks,
        inner_x[0], inner_bc[0], step_size[0],
        decay_base[None, :], conv_inner, conv_groups, norm_gain[None, :],
        cache_pool,
    )
    return result[None]


def solution(mesh):
    return jax.shard_map(
        functools.partial(body, mesh.shape["batch"], mesh.shape["ctx"]),
        mesh=mesh,
        in_specs=(
            P("batch", "ctx", None),
            P("batch", "ctx", None),
            P("batch", "ctx", None),
            P(),
            P(),
            P(),
            P(),
            P("batch", "ctx", None, None),
            P(),
            P(),
            P(),
        ),
        out_specs=P("batch", "ctx", None),
        check_vma=False,
    )
```

time: 78 us -> 69.6 us (0.89)
  local copies, waits for them, and re-layouts: 6.76 us -> 2.26 us
  Pallas kernels: 70.8 us -> 67.1 us
    unnamed x24 -> x1, local copies, waits for them, and re-layouts: 6.01 us -> 2.26 us
    pallas_call x1, Pallas kernels: 70.8 us -> 67.1 us  [body(): pl.pallas_call(functools.partial(kernel, nb, nc, length), out_shape=jax.S...]
where the time goes in v2:
time: 69.6 us; the launch traced here: 69.4 us
  Pallas kernels  67.1 us (96%)
  local copies, waits for them, and re-layouts  2.26 us (3%)
    pallas_call x1, Pallas kernels, body(): pl.pallas_call(functools.partial(kernel, nb, nc, length), out_shape=jax.S...  67.1 us
    unnamed x1, local copies, waits for them, and re-layouts  2.26 us

profile of v2, /device:TPU:25, one launch (start us, length us, event | category | flops | bytes accessed | tf_op | source)
XLA Modules:
  0.0 69.4 jit_solution(8131396544530315807)
XLA Ops:
  0.0 67.1 %shard_map.109 = bf16[64,8192]{1,0:T(8,128)(2,1)} custom-call(s32[4]{0:T(128)} %owner_ref.1, s32[4]{0:T(128)} %level_ref.1, s32[4]{0:T(128)} %blocks_ref.1, bf16[64,8192]{1,0:T(8,128)(2,1)} %bitcast.7, bf16[64,1024]{1,0:T(8,128)(2,1)} %bitcast.8, f32[64,64]{1,0:T(8,128)} %bitcast.9, f32[1,64]{1,0:T(1,128)} %bitcast.11, f32[4,8192]{1,0:T(4,128)} %wx_hbm.1, ...), custom_call_target="tpu_custom_call" | custom-call | tf_op jit(solution)/shard_map/pallas_call | solution.py:307
  67.2 2.3 %copy.13 = bf16[1,64,8192]{2,1,0:T(8,128)(2,1)} copy(bf16[1,64,8192]{2,1,0:T(8,128)(2,1)} %bitcast.6) | data formatting | bytes 2097152

commit v3 on v2

--- a/solution.py
+++ b/solution.py
@@ -14,7 +14,7 @@
 KCONV = 4
 LEN_BLOCK = 256
 HALO = 16
-PARTS = 2
+PARTS = 4
 F32 = jnp.float32
 BF16 = jnp.bfloat16
 MESH = pl.DeviceIdType.MESH
@@ -48,7 +48,9 @@
 ):
     hs = LOCAL_HEADS // nc
     width = hs * P_SIZE
-    sub = width // PARTS
+    parts = min(PARTS, hs)
+    share = hs // parts
+    sub = width // parts
     per_group = LOCAL_HEADS // GROUPS
     me_b = lax.axis_index("batch")
     me_c = lax.axis_index("ctx")
@@ -85,15 +87,18 @@
             device_id=(me_b, lax.rem(me_c + 1, nc)), device_id_type=MESH,
         )
 
-    def sel_copy(step):
+    def rows_of(part):
+        return pl.ds(pl.multiple_of(part * sub, P_SIZE), sub)
+
+    def sel_copy(step, part):
         return pltpu.make_async_remote_copy(
-            src_ref=sel_out.at[step - 1], dst_ref=sel_in.at[step - 1],
-            send_sem=sel_send.at[step - 1], recv_sem=sel_recv.at[step - 1],
+            src_ref=sel_out.at[step - 1, rows_of(part)], dst_ref=sel_in.at[step - 1, rows_of(part)],
+            send_sem=sel_send.at[step - 1, part], recv_sem=sel_recv.at[step - 1, part],
             device_id=(lax.rem(me_b + step, nb), me_c), device_id_type=MESH,
         )
 
     def start_copy(part):
-        rows = pl.ds(part * sub, sub)
+        rows = rows_of(part)
         return pltpu.make_async_remote_copy(
             src_ref=start.at[rows], dst_ref=inc.at[me_c, rows],
             send_sem=st_send.at[part], recv_sem=inc_recv.at[me_c, part],
@@ -101,7 +106,7 @@
         )
 
     def next_copy(k, part):
-        rows = pl.ds(part * sub, sub)
+        rows = rows_of(part)
         return pltpu.make_async_remote_copy(
             src_ref=nxt.at[k, rows], dst_ref=inc.at[k, rows],
             send_sem=nxt_send.at[k, part], recv_sem=inc_recv.at[k, part],
@@ -113,8 +118,9 @@
         halo_copy(1).start()
         halo_copy(0).start()
 
-    for step in range(1, nb):
-        sel_copy(step).start()
+    for part in range(parts):
+        for step in range(1, nb):
+            sel_copy(step, part).start()
 
     first = me_c * length
     row_at = lax.broadcasted_iota(jnp.int32, (length, LOCAL_HEADS), 0)
@@ -184,98 +190,106 @@
             mixing = (scores * jnp.exp(gap) * row_i[j : j + 1]).astype(BF16)
             intra[k, :, lanes] = jnp.dot(mixing, convs[k, :, lanes], preferred_element_type=F32)
 
-    def start_part():
+    def start_part(part):
         owner = owner_ref[me_b]
         level = level_ref[me_b]
+        rows = rows_of(part)
         for step in range(1, nb):
-            sel_copy(step).wait_recv()
-        state = jnp.where(owner == me_b, start[...], jnp.zeros_like(start))
+            sel_copy(step, part).wait_recv()
+        mine = start[rows]
+        state = jnp.where(owner == me_b, mine, jnp.zeros_like(mine))
         for step in range(1, nb):
-            state = jnp.where(owner == lax.rem(me_b + nb - step, nb), sel_in[step - 1], state)
+            state = jnp.where(owner == lax.rem(me_b + nb - step, nb), sel_in[step - 1, rows], state)
         state = jnp.where(level > 0, state, jnp.zeros_like(state))
 
         @pl.when(me_c == 0)
         def _():
-            inc[0] = state
+            inc[0, rows] = state
 
         @pl.when(me_c > 0)
         def _():
-            start[...] = state
-            for part in range(PARTS):
-                start_copy(part).start()
-
-    def chain_part(k):
-        decay = jnp.exp(rowc[k][:, length - 1 : length]).astype(BF16).astype(F32)
-        for part in range(PARTS):
-            @pl.when(me_c + k > 0)
-            def _():
-                next_copy(k, part).wait_recv()
-
-            @pl.when(me_c < nc - 1)
-            def _():
-                for j in range(part * hs // PARTS, (part + 1) * hs // PARTS):
-                    rows = slice(j * P_SIZE, (j + 1) * P_SIZE)
-                    nxt[k, rows] = (
-                        decay[j : j + 1] * inc[k, rows].astype(F32) + ends[k, rows].astype(F32)
-                    ).astype(BF16)
-                next_copy(k, part).start()
-
-    def out_part(k):
+            start[rows] = state
+            start_copy(part).start()
+
+    def chain_part(k, part):
+        @pl.when(me_c + k > 0)
+        def _():
+            next_copy(k, part).wait_recv()
+
+        @pl.when(me_c < nc - 1)
+        def _():
+            decay = jnp.exp(rowc[k][:, length - 1 : length]).astype(BF16).astype(F32)
+            for j in range(part * share, (part + 1) * share):
+                rows = slice(j * P_SIZE, (j + 1) * P_SIZE)
+                nxt[k, rows] = (
+                    decay[j : j + 1] * inc[k, rows].astype(F32) + ends[k, rows].astype(F32)
+                ).astype(BF16)
+            next_copy(k, part).start()
+
+    def out_part(k, part):
         read = bcv[GROUPS + k * hs // per_group]
-        inter = lax.dot_general(read, inc[k], NT, preferred_element_type=F32)
+        inter = lax.dot_general(
+            read, inc[k, part * sub : (part + 1) * sub], NT, preferred_element_type=F32
+        )
         grown = jnp.exp(colc[k])
-        gain = gain_ref[:, columns(k)]
+        cols = pl.ds(pl.multiple_of(k * width + part * sub, P_SIZE), sub)
+        gain = gain_ref[:, cols]
         alive = first + lax.broadcasted_iota(jnp.int32, (length, P_SIZE), 0) < live_count
         outs = []
-        for j in range(hs):
-            lanes = slice(j * P_SIZE, (j + 1) * P_SIZE)
-            summed = intra[k, :, lanes] + grown[:, j : j + 1] * inter[:, lanes]
+        for at in range(share):
+            j = part * share + at
+            lanes = slice(at * P_SIZE, (at + 1) * P_SIZE)
+            summed = (
+                intra[k, :, j * P_SIZE : (j + 1) * P_SIZE] + grown[:, j : j + 1] * inter[:, lanes]
+            )
             scale = lax.rsqrt(jnp.mean(summed * summed, axis=1, keepdims=True) + 1e-05)
             outs.append(jnp.where(alive, summed * scale * gain[:, lanes], 0.0).astype(BF16))
-        out_ref[:, columns(k)] = jnp.concatenate(outs, axis=1)
-
-    start_at = jnp.where(me_c == 0, 0, nc // 2 - 1)
+        out_ref[:, cols] = jnp.concatenate(outs, axis=1)
 
     def ends_step(k, carry):
         end_part(k)
-        pl.when(k == start_at)(start_part)
-
-        @pl.when(me_c == 0)
-        def _():
-            chain_part(k)
-
         return carry
 
     def intra_step(k, carry):
         intra_part(k)
         return carry
 
-    def late_step(k, carry):
-        @pl.when(me_c > 0)
-        def _():
-            chain_part(k)
-
-        @pl.when(me_c < 2)
-        def _():
-            intra_part(k)
-
-        out_part(k)
+    def late_step(part, k, carry):
+        def serve(later, inner):
+            @pl.when(part * nc + k == jnp.maximum(6 * later - 2 * me_c, 0))
+            def _():
+                start_part(later)
+
+            return inner
+
+        if part < parts - 1:
+            lax.fori_loop(1, parts, serve, 0)
+        chain_part(k, part)
+        if part == 0:
+            @pl.when(me_c < 2)
+            def _():
+                intra_part(k)
+
+        out_part(k, part)
         return carry
 
     lax.fori_loop(0, nc, ends_step, 0)
+    start_part(0)
 
     @pl.when(me_c >= 2)
     def _():
         lax.fori_loop(0, nc, intra_step, 0)
 
-    lax.fori_loop(0, nc, late_step, 0)
-
-    for step in range(1, nb):
-        sel_copy(step).wait_send()
+    for part in range(parts):
+        lax.fori_loop(0, nc, functools.partial(late_step, part), 0)
+
+    for part in range(parts):
+        for step in range(1, nb):
+            sel_copy(step, part).wait_send()
 
     @pl.when(me_c > 0)
     def _():
-        for part in range(PARTS):
+        for part in range(parts):
             start_copy(part).wait_send()
 
     @pl.when(me_c < nc - 1)
@@ -284,7 +298,7 @@
         halo_copy(0).wait_send()
 
         def drain(k, carry):
-            for part in range(PARTS):
+            for part in range(parts):
                 next_copy(k, part).wait_send()
             return carry
 
@@ -300,6 +314,7 @@
     width_bc = inner_bc.shape[2]
     hs = LOCAL_HEADS // nc
     width = hs * P_SIZE
+    parts = min(PARTS, hs)
     smem = pl.BlockSpec(memory_space=pltpu.SMEM)
     vmem = pl.BlockSpec(memory_space=pltpu.VMEM)
     hbm = pl.BlockSpec(memory_space=pl.ANY)
@@ -332,11 +347,11 @@
             dma((3,)),
             dma((2,)),
             dma((2,)),
-            dma((nb - 1,)),
-            dma((nb - 1,)),
-            dma((PARTS,)),
-            dma((nc, PARTS)),
-            dma((nc, PARTS)),
+            dma((nb - 1, parts)),
+            dma((nb - 1, parts)),
+            dma((parts,)),
+            dma((nc, parts)),
+            dma((nc, parts)),
         ],
         compiler_params=pltpu.CompilerParams(
             collective_id=0, has_side_effects=True, vmem_limit_bytes=56 * 1024 * 1024

time: 69.6 us -> 59.6 us (0.86)
  Pallas kernels: 67.1 us -> 57.2 us
    pallas_call x1, Pallas kernels: 67.1 us -> 57.2 us  [body(): pl.pallas_call(functools.partial(kernel, nb, nc, length), out_shape=jax.S...]
where the time goes in v3:
time: 59.6 us; the launch traced here: 59.4 us
  Pallas kernels  57.2 us (96%)
  local copies, waits for them, and re-layouts  2.26 us (4%)
    pallas_call x1, Pallas kernels, body(): pl.pallas_call(functools.partial(kernel, nb, nc, length), out_shape=jax.S...  57.2 us
    unnamed x1, local copies, waits for them, and re-layouts  2.26 us

profile of v3, /device:TPU:25, one launch (start us, length us, event | category | flops | bytes accessed | tf_op | source)
XLA Modules:
  0.0 59.4 jit_solution(6621698474087346318)
XLA Ops:
  0.0 57.2 %shard_map.109 = bf16[64,8192]{1,0:T(8,128)(2,1)} custom-call(s32[4]{0:T(128)} %owner_ref.1, s32[4]{0:T(128)} %level_ref.1, s32[4]{0:T(128)} %blocks_ref.1, bf16[64,8192]{1,0:T(8,128)(2,1)} %bitcast.7, bf16[64,1024]{1,0:T(8,128)(2,1)} %bitcast.8, f32[64,64]{1,0:T(8,128)} %bitcast.9, f32[1,64]{1,0:T(1,128)} %bitcast.11, f32[4,8192]{1,0:T(4,128)} %wx_hbm.1, ...), custom_call_target="tpu_custom_call" | custom-call | tf_op jit(solution)/shard_map/pallas_call | solution.py:322
  57.2 2.3 %copy.13 = bf16[1,64,8192]{2,1,0:T(8,128)(2,1)} copy(bf16[1,64,8192]{2,1,0:T(8,128)(2,1)} %bitcast.6) | data formatting | bytes 2097152

commit v4 on v3

--- a/solution.py
+++ b/solution.py
@@ -40,9 +40,9 @@
 def kernel(
     nb, nc, length,
     owner_ref, level_ref, blocks_ref,
-    x_hbm, bc_ref, step_ref, base_ref, wx_hbm, wbc_ref, gain_ref, pool_hbm,
-    out_ref,
-    x_ref, wx_ref, pool_ref, convs,
+    x_hbm, bc_hbm, step_ref, base_ref, wx_hbm, wbc_hbm, gain_hbm, pool_hbm,
+    out_hbm,
+    x_ref, wx_ref, pool_ref, convs, bc_ref, wbc_ref, gain_ref, out_ref, out_sem,
     hx, hbc, ext, bcv, colc, coli, rowc, rowi, intra, ends, inc, nxt, sel_out, sel_in, start,
     local_sem, halo_send, halo_recv, sel_send, sel_recv, st_send, inc_recv, nxt_send,
 ):
@@ -58,7 +58,10 @@
 
     loads = [
         pltpu.make_async_copy(source, target, local_sem.at[at])
-        for at, (source, target) in enumerate(((pool_hbm, pool_ref), (x_hbm, x_ref), (wx_hbm, wx_ref)))
+        for at, (source, target) in enumerate((
+            (pool_hbm, pool_ref), (x_hbm, x_ref), (bc_hbm, bc_ref),
+            (wbc_hbm, wbc_ref), (wx_hbm, wx_ref), (gain_hbm, gain_ref),
+        ))
     ]
     for load in loads:
         load.start()
@@ -77,6 +80,7 @@
         sel_out[step - 1] = pick(lax.rem(me_b + step, nb))
     start[...] = pick(me_b)
     loads[1].wait()
+    loads[2].wait()
     pl.semaphore_wait(barrier, nb - 1 + nc - 1)
 
     def halo_copy(which):
@@ -152,6 +156,7 @@
         halo_copy(1).wait_recv()
         halo_copy(0).wait_recv()
 
+    loads[3].wait()
     half = GROUPS * N
     for part in range(2):
         cols = slice(part * half, (part + 1) * half)
@@ -161,7 +166,8 @@
             ext[8 : 8 + length, :N] = bc_ref[:, at : at + N].astype(F32)
             bcv[part * GROUPS + piece] = convolved(ext, wbc_ref[:, at : at + N], length, N)
 
-    loads[2].wait()
+    loads[4].wait()
+    loads[5].wait()
 
     def columns(k):
         return pl.ds(pl.multiple_of(k * width, 128), width)
@@ -225,6 +231,10 @@
                     decay[j : j + 1] * inc[k, rows].astype(F32) + ends[k, rows].astype(F32)
                 ).astype(BF16)
             next_copy(k, part).start()
+
+    def out_copy(k, part):
+        cols = pl.ds(pl.multiple_of(k * width + part * sub, P_SIZE), sub)
+        return pltpu.make_async_copy(out_ref.at[:, cols], out_hbm.at[:, cols], out_sem.at[k, part])
 
     def out_part(k, part):
         read = bcv[GROUPS + k * hs // per_group]
@@ -245,6 +255,7 @@
             scale = lax.rsqrt(jnp.mean(summed * summed, axis=1, keepdims=True) + 1e-05)
             outs.append(jnp.where(alive, summed * scale * gain[:, lanes], 0.0).astype(BF16))
         out_ref[:, cols] = jnp.concatenate(outs, axis=1)
+        out_copy(k, part).start()
 
     def ends_step(k, carry):
         end_part(k)
@@ -303,6 +314,13 @@
             return carry
 
         lax.fori_loop(0, nc, drain, 0)
+
+    def finish(k, carry):
+        for part in range(parts):
+            out_copy(k, part).wait()
+        return carry
+
+    lax.fori_loop(0, nc, finish, 0)
 
 
 def body(
@@ -322,13 +340,18 @@
     result = pl.pallas_call(
         functools.partial(kernel, nb, nc, length),
         out_shape=jax.ShapeDtypeStruct((length, width_x), BF16),
-        in_specs=[smem] * 3 + [hbm, vmem, vmem, vmem, hbm, vmem, vmem, hbm],
-        out_specs=vmem,
+        in_specs=[smem] * 3 + [hbm, hbm, vmem, vmem, hbm, hbm, hbm, hbm],
+        out_specs=hbm,
         scratch_shapes=[
             pltpu.VMEM((length, width_x), BF16),
             pltpu.VMEM((KCONV, width_x), F32),
             pltpu.VMEM(cache_pool.shape, BF16),
             pltpu.VMEM((nc, length, width), BF16),
+            pltpu.VMEM((length, width_bc), BF16),
+            pltpu.VMEM((KCONV, width_bc), F32),
+            pltpu.VMEM((1, width_x), F32),
+            pltpu.VMEM((length, width_x), BF16),
+            dma((nc, parts)),
             pltpu.VMEM((HALO, width_x), BF16),
             pltpu.VMEM((HALO, width_bc), BF16),
             pltpu.VMEM((8 + length, max(width, N)), F32),
@@ -344,7 +367,7 @@
             pltpu.VMEM((nb - 1, width, N), BF16),
             pltpu.VMEM((nb - 1, width, N), BF16),
             pltpu.VMEM((width, N), BF16),
-            dma((3,)),
+            dma((6,)),
             dma((2,)),
             dma((2,)),
             dma((nb - 1, parts)),

time: 59.6 us -> 59.4 us (level)
  no operation moved by 1% of the time
where the time goes in v4:
time: 59.4 us; the launch traced here: 59.2 us
  Pallas kernels  56.9 us (96%)
  local copies, waits for them, and re-layouts  2.26 us (4%)
    pallas_call x1, Pallas kernels, body(): pl.pallas_call(functools.partial(kernel, nb, nc, length), out_shape=jax.S...  56.9 us
    unnamed x1, local copies, waits for them, and re-layouts  2.26 us

profile of v4, /device:TPU:25, one launch (start us, length us, event | category | flops | bytes accessed | tf_op | source)
XLA Modules:
  0.0 59.2 jit_solution(16775643436704207597)
XLA Ops:
  0.0 56.9 %shard_map.109 = bf16[64,8192]{1,0:T(8,128)(2,1)} custom-call(s32[4]{0:T(128)} %owner_ref.1, s32[4]{0:T(128)} %level_ref.1, s32[4]{0:T(128)} %blocks_ref.1, bf16[64,8192]{1,0:T(8,128)(2,1)} %bitcast.7, bf16[64,1024]{1,0:T(8,128)(2,1)} %bitcast.8, f32[64,64]{1,0:T(8,128)} %bitcast.9, f32[1,64]{1,0:T(1,128)} %bitcast.11, f32[4,8192]{1,0:T(4,128)} %wx_hbm.1, ...), custom_call_target="tpu_custom_call" | custom-call | tf_op jit(solution)/shard_map/pallas_call | solution.py:340
  56.9 2.3 %copy.13 = bf16[1,64,8192]{2,1,0:T(8,128)(2,1)} copy(bf16[1,64,8192]{2,1,0:T(8,128)(2,1)} %bitcast.6) | data formatting | bytes 2097152
